TPU v7x, 32 devices: a whole 2x2x4 slice. The times are simulated.
32 devices in a mesh: seq: 4 (over y, x), tensor: 8 (over z, core).
Axes of the slice: x: 2, y: 2, z: 4, core: 2. Of those that a mesh axis runs over, the one named last changes fastest.
Arguments:
- hidden: bfloat16 [64, 2048], P('seq', 'tensor'), may hold values from -6 to 6
- router_logits: float32 [64, 8], replicated, may hold values from -6 to 6
- routes: int32 [64, 2], replicated, may hold values from 0 to 7, all different within a row
- w_query: bfloat16 [8, 2048, 2048], P(None, 'tensor', 'seq'), may hold values from -0.125 to 0.125
- w_keyval: bfloat16 [2048, 2, 2048], P('tensor', None, 'seq'), may hold values from -0.125 to 0.125
- w_output: bfloat16 [8, 2048, 2048], P(None, 'seq', 'tensor'), may hold values from -0.125 to 0.125
- k_cache: bfloat16 [1024, 64, 2048], P(('seq', 'tensor')), may hold values from -720 to 720
- v_cache: bfloat16 [1024, 64, 2048], P(('seq', 'tensor')), may hold values from -6 to 6
- lengths: int32 [16], replicated, may hold values from 1 to 4096, 26214 in all
- page_table: int32 [16, 64], replicated, may hold values from 0 to 31, as said below
- home_device: int32 [16], replicated, may hold values from 0 to 3
- accepted: int32 [16], replicated, may hold values from 1 to 4
Outputs:
- attn_out: float32 [64, 2048], P('seq', 'tensor')
- new_keys: float32 [64, 2048], P('tensor', 'seq')
- new_values: float32 [64, 2048], P('tensor', 'seq')
Inputs may be any that keep to these rules, and one draw needn't show every extreme that they name: `page_table`: for each index s of seq and t of tensor, the pages j of the requests r with r // 2 = t and (home_device[r] + j) % 4 = s have distinct values.
All inputs are finite; a program needn't handle non-finite values.
Results may differ from a plain program's by a relative error of at most 0.019.
Values may be sent and summed in bfloat16 or wider, within the bound.
No kernel may reach another device: no remote copies, remote signals or barrier semaphores. Data moves between devices by JAX's collectives and lax.ppermute only.
A program may use at most 128 MiB of HBM per device.

v0:
```python
import math

import jax
import jax.numpy as jnp
from jax import lax
from jax.sharding import PartitionSpec as P

HD = 128
Q = 4
PAGE = 64
MAXP = 64


THETA = 10000.0
NEGATIVE = -1e30


def joined_2(part, axis, combine):
    gathered = jax.tree.map(lambda a: lax.all_gather(a, axis), part)

    def take(source):
        return jax.tree.map(lambda a: lax.dynamic_index_in_dim(a, source, 0, False), gathered)

    return lax.fori_loop(
        1, lax.axis_size(axis), lambda source, state: combine(state, take(source)), take(0)
    )


def rotate(vectors, positions):
    half_width = HD // 2
    inverse = THETA ** (-(jnp.arange(half_width, dtype=jnp.float32) * 2.0 / HD))
    angles = positions.astype(jnp.float32)[..., None] * inverse
    cosine = jnp.cos(angles)
    sine_vals = jnp.sin(angles)
    front_half = vectors[..., :half_width]
    back_half = vectors[..., half_width:]
    return jnp.concatenate(
        [front_half * cosine - back_half * sine_vals, back_half * cosine + front_half * sine_vals],
        axis=-1,
    )


def combine(earlier, later):
    top_one, sums_one, accum_one = earlier
    top_two, sums_two, accum_two = later
    top_score = jnp.maximum(top_one, top_two)
    factor_one = jnp.exp(top_one - top_score)
    factor_two = jnp.exp(top_two - top_score)
    return (
        top_score,
        sums_one * factor_one + sums_two * factor_two,
        accum_one * factor_one[..., None] + accum_two * factor_two[..., None],
    )


def per_device(
    hidden,
    router_logits,
    routes,
    w_query,
    w_keyval,
    w_output,
    k_cache,
    v_cache,
    lengths,
    page_table,
    home_device,
    accepted,
):
    seq_count = lax.axis_size("seq")
    tensor_count = lax.axis_size("tensor")
    seq_index = lax.axis_index("seq")
    tensor_index = lax.axis_index("tensor")
    tok_total = routes.shape[0]
    tok_own = tok_total // tensor_count
    req_own = tok_own // Q
    experts = w_query.shape[0]
    local_width = w_query.shape[2]
    heads_here = local_width // HD
    kv_heads = heads_here * seq_count
    scaling = 1.0 / math.sqrt(HD)
    selector = routes[:, :, None] == jnp.arange(experts, dtype=jnp.int32)[None, None, :]
    columns = lax.all_gather(hidden, "seq", axis=0, tiled=True)
    picked = selector
    query_every = jnp.einsum("nd,edh->neh", columns, w_query, preferred_element_type=jnp.float32)
    query_two = jnp.sum(jnp.where(picked[:, :, :, None], query_every[:, None, :, :], 0.0), axis=2)
    keyval = jnp.einsum("nd,dch->nch", columns, w_keyval, preferred_element_type=jnp.float32)
    summed = lax.psum(jnp.concatenate([query_two, keyval], axis=1), "tensor")
    owned = lax.dynamic_slice_in_dim(summed, tensor_index * tok_own, tok_own, 0)
    lens_own = lax.dynamic_slice_in_dim(lengths, tensor_index * req_own, req_own, 0)
    homes_own = lax.dynamic_slice_in_dim(home_device, tensor_index * req_own, req_own, 0)
    accept_own = lax.dynamic_slice_in_dim(accepted, tensor_index * req_own, req_own, 0)
    steps_own = jnp.arange(tok_own, dtype=jnp.int32) % Q
    positions = jnp.repeat(lens_own, Q) + steps_own
    queries = rotate(
        owned[:, :2].reshape(tok_own, 2, heads_here, HD), positions[:, None, None]
    ).astype(jnp.bfloat16)
    keys_rotated = rotate(owned[:, 2].reshape(tok_own, heads_here, HD), positions[:, None])
    values_raw = owned[:, 3].reshape(tok_own, heads_here, HD)
    keys_fresh = keys_rotated.astype(jnp.bfloat16)
    values_fresh = values_raw.astype(jnp.bfloat16)
    queries_all = lax.all_gather(queries, "seq", axis=2, tiled=True)
    pages_here = MAXP // seq_count
    tables_own = lax.dynamic_slice_in_dim(page_table, tensor_index * req_own, req_own, 0)
    offsets = (seq_index - homes_own) % seq_count
    logical = offsets[:, None] + seq_count * jnp.arange(pages_here, dtype=jnp.int32)[None, :]
    slots = jnp.take_along_axis(tables_own, logical, axis=1)
    key_count = pages_here * PAGE
    cache_keys = k_cache[slots].reshape(req_own, key_count, kv_heads, HD)
    cache_values = v_cache[slots].reshape(req_own, key_count, kv_heads, HD)
    key_positions = (
        logical[:, :, None] * PAGE + jnp.arange(PAGE, dtype=jnp.int32)[None, None, :]
    ).reshape(req_own, key_count)
    valid = (key_positions < lens_own[:, None])[:, None, None, None, :]
    query_blocks = queries_all.reshape(req_own, Q, 2, kv_heads, HD)
    scores = (
        jnp.einsum(
            "rqkhd,rlhd->rqkhl", query_blocks, cache_keys, preferred_element_type=jnp.float32
        )
        * scaling
    )
    scores = jnp.where(valid, scores, NEGATIVE)
    top_local = jnp.max(scores, axis=-1)
    weights = jnp.where(valid, jnp.exp(scores - top_local[..., None]), 0.0)
    sums_local = jnp.sum(weights, axis=-1)
    accum_local = jnp.einsum(
        "rqkhl,rlhd->rqkhd",
        weights.astype(jnp.bfloat16),
        cache_values,
        preferred_element_type=jnp.float32,
    )
    merged = joined_2((top_local, sums_local, accum_local), "seq", combine)
    top_cache = lax.dynamic_slice_in_dim(merged[0], seq_index * heads_here, heads_here, 3)
    sums_cache = lax.dynamic_slice_in_dim(merged[1], seq_index * heads_here, heads_here, 3)
    accum_cache = lax.dynamic_slice_in_dim(merged[2], seq_index * heads_here, heads_here, 3)
    own_queries = queries.reshape(req_own, Q, 2, heads_here, HD)
    own_keys = keys_fresh.reshape(req_own, Q, heads_here, HD)
    own_values = values_fresh.reshape(req_own, Q, heads_here, HD)
    causal = (jnp.arange(Q, dtype=jnp.int32)[:, None] >= jnp.arange(Q, dtype=jnp.int32)[None, :])[
        None, :, None, None, :
    ]
    fresh_scores = (
        jnp.einsum("rqkhd,rthd->rqkht", own_queries, own_keys, preferred_element_type=jnp.float32)
        * scaling
    )
    fresh_scores = jnp.where(causal, fresh_scores, NEGATIVE)
    top_fresh = jnp.max(fresh_scores, axis=-1)
    fresh_weights = jnp.where(causal, jnp.exp(fresh_scores - top_fresh[..., None]), 0.0)
    sums_fresh = jnp.sum(fresh_weights, axis=-1)
    accum_fresh = jnp.einsum(
        "rqkht,rthd->rqkhd",
        fresh_weights.astype(jnp.bfloat16),
        own_values,
        preferred_element_type=jnp.float32,
    )
    joined = combine((top_cache, sums_cache, accum_cache), (top_fresh, sums_fresh, accum_fresh))
    attended = (
        (joined[2] / joined[1][..., None]).astype(jnp.bfloat16).reshape(tok_own, 2, local_width)
    )
    chosen = jnp.sum(jnp.where(selector, router_logits[:, None, :], 0.0), axis=2)
    gate_probs = jax.nn.softmax(chosen, axis=1)
    picked = selector
    projected = jnp.einsum(
        "nkh,ehd->nked",
        lax.all_gather(attended, "tensor", axis=0, tiled=True),
        w_output,
        preferred_element_type=jnp.float32,
    )
    mixing = jnp.where(picked, gate_probs[:, :, None], 0.0)
    partial_out = jnp.sum(mixing[..., None] * projected, axis=(1, 2))
    out_rows = lax.psum_scatter(partial_out, "seq", scatter_dimension=0, tiled=True)
    rows_here = tok_total // seq_count
    global_rows = seq_index * rows_here + jnp.arange(rows_here, dtype=jnp.int32)
    kept_rows = global_rows % Q < jnp.take(accepted, global_rows // Q)
    attn_out = jnp.where(kept_rows[:, None], out_rows, 0.0)
    kept_own = steps_own < jnp.repeat(accept_own, Q)
    new_keys = jnp.where(kept_own[:, None], keys_rotated.reshape(tok_own, local_width), 0.0)
    new_values = jnp.where(kept_own[:, None], values_raw.reshape(tok_own, local_width), 0.0)
    return (attn_out, new_keys, new_values)


def solution(mesh):
    in_specs = (
        P("seq", "tensor"),
        P(),
        P(),
        P(None, "tensor", "seq"),
        P("tensor", None, "seq"),
        P(None, "seq", "tensor"),
        P(("seq", "tensor"), None, None),
        P(("seq", "tensor"), None, None),
        P(),
        P(),
        P(),
        P(),
    )
    out_specs = (P("seq", "tensor"), P("tensor", "seq"), P("tensor", "seq"))
    return jax.shard_map(
        per_device, mesh=mesh, in_specs=in_specs, out_specs=out_specs, check_vma=False
    )
```

profile of v0, /device:TPU:0, one launch (start us, length us, event | category | flops | bytes accessed | tf_op | source)
XLA Modules:
  0.0 181.2 jit_solution(9389079777092124582)
XLA Ops:
  7.2 9.9 %all_gather.27 = bf16[64,256]{1,0:T(8,128)(2,1)S(1)} all-gather(bf16[16,256]{1,0:T(8,128)(2,1)} %param.14), channel_id=1, replica_groups=mesh['seq'=4,'tensor'=8] {'seq'}, dimensions={0}, use_global_device_ids=true | all-gather | bytes 40960 | tf_op jit(solution)/shard_map/all_gather | solution.py:83
  17.1 0.5 fusion.45
  17.6 0.6 copy.81
  18.2 0.7 iota_compare_fusion
  18.9 0.1 copy.80
  19.1 0.8 select_reduce_fusion
  19.9 1.2 fusion.37
  21.2 0.9 pad_maximum_fusion
  22.1 0.2 reduce-scatter.2.cloned.1.call-start
  22.4 0.1 and_select_fusion.2
  22.8 0.1 reshape.566
  22.9 0.7 constant_dynamic-slice_fusion.2
  23.6 0.8 gather_fusion.3
  24.6 8.4 %gather_fusion.1 = bf16[32,64,2048]{2,1,0:T(8,128)(2,1)} fusion(bf16[32,64,2048]{2,1,0:T(8,128)(2,1)} %param.20, s32[1024]{0:T(1024)S(1)} %pad_clamp_fusion), kind=kCustom, calls=%fused_computation.1 | custom fusion | bytes 16777344 | tf_op jit(solution)/shard_map/gather | solution.py:109
  33.1 9.8 %copy.126 = bf16[256,8,16,128]{3,2,1,0:T(8,128)(2,1)} copy(bf16[256,8,16,128]{3,1,2,0:T(8,128)(2,1)} %bitcast.110) | data formatting | bytes 16777216
  42.9 8.1 %bitcast_bitcast_fusion.1 = bf16[2,1024,16,128,1]{3,2,1,0,4:T(8,128)(2,1)} fusion(bf16[2,1024,16,128]{3,2,1,0:T(8,128)(2,1)} %bitcast.107), kind=kLoop, calls=%fused_computation.16 | loop fusion | bytes 16777216 | tf_op jit(solution)/shard_map/reshape | solution.py:109
  50.9 8.4 %gather_fusion.2 = bf16[32,64,2048]{2,1,0:T(8,128)(2,1)} fusion(bf16[32,64,2048]{2,1,0:T(8,128)(2,1)} %param.21, s32[1024]{0:T(1024)S(1)} %pad_clamp_fusion), kind=kCustom, calls=%fused_computation.2 | custom fusion | bytes 16777344 | tf_op jit(solution)/shard_map/gather | solution.py:110
  59.3 9.8 %copy.127 = bf16[256,8,16,128]{3,2,1,0:T(8,128)(2,1)} copy(bf16[256,8,16,128]{3,1,2,0:T(8,128)(2,1)} %bitcast.108) | data formatting | bytes 16777216
  69.1 8.1 %bitcast_bitcast_fusion = bf16[2,1024,16,128,1]{3,2,1,0,4:T(8,128)(2,1)} fusion(bf16[2,1024,16,128]{3,2,1,0:T(8,128)(2,1)} %bitcast.109), kind=kLoop, calls=%fused_computation.15 | loop fusion | bytes 16777216 | tf_op jit(solution)/shard_map/reshape | solution.py:110
  77.4 0.7 gather_fusion
  78.2 0.1 reshape.570
  78.3 0.1 multiply_cosine_fusion
  78.7 0.8 dynamic-slice_bitcast_fusion
  79.7 8.4 %all_gather.28 = bf16[8,2,16,128]{3,0,1,2:T(8,128)(2,1)S(1)} all-gather(bf16[8,2,4,128]{3,0,1,2:T(8,128)(2,1)S(1)} %copy.84), channel_id=1, replica_groups=mesh['seq'=4,'tensor'=8] {'seq'}, dimensions={2}, use_global_device_ids=true | all-gather | bytes 81920 | tf_op jit(solution)/shard_map/all_gather | solution.py:102
  88.0 7.8 %fusion.73 = (f32[2,4,2,16]{1,2,3,0:T(2,128)S(1)}, f32[2,4,2,16,1024]{4,1,2,3,0:T(4,128)S(1)}) fusion(bf16[2,4,2,16,128]{4,1,0,2,3:T(4,128)(2,1)S(1)} %bitcast.114, bf16[2,1024,16,128,1]{3,2,1,0,4:T(8,128)(2,1)} %bitcast_bitcast_fusion.1, pred[2,1024]{1,0:T(4,128)(4,1)S(1)} %add_compare_fusion), kind=kOutput, calls=%fused_computation.125 | convolution fusion | flops 67895040 | bytes 9505792 | tf_op jit(solution)/shard_map/rqkhd,rlhd->rqkhl/dot_general | solution.py:117
  95.8 0.1 copy.88
  95.9 0.6 fusion.35
  96.5 7.8 %fusion.19 = f32[2,4,2,16,128]{4,1,2,3,0:T(4,128)S(1)} fusion(bf16[2,1024,16,128,1]{3,2,1,0,4:T(8,128)(2,1)} %bitcast_bitcast_fusion, f32[2,4,2,16,1024]{4,1,2,3,0:T(4,128)S(1)} %get-tuple-element.248, f32[2,4,2,16]{1,2,3,0:T(2,128)S(1)} %get-tuple-element.247, pred[2,1024]{1,0:T(4,128)(4,1)S(1)} %add_compare_fusion), kind=kOutput, calls=%fused_computation.27 | convolution fusion | flops 67895296 | bytes 9571328 | tf_op jit(solution)/shard_map/rqkhl,rlhd->rqkhd/dot_general | solution.py:126
  104.3 10.1 %all-gather.2 = f32[8,4,2,16,128]{4,3,2,1,0:T(8,128)S(1)} all-gather(f32[2,4,2,16,128]{4,3,2,1,0:T(8,128)S(1)} %copy.91), channel_id=4, replica_groups=mesh['seq'=4,'tensor'=8] {'seq'}, dimensions={0}, use_global_device_ids=true | all-gather | bytes 655360 | tf_op jit(solution)/shard_map/all_gather | solution.py:19
  114.4 0.1 copy.89
  114.5 7.1 %all-gather.1 = f32[8,4,2,16]{3,1,2,0:T(4,128)S(1)} all-gather(f32[2,4,2,16]{3,1,2,0:T(4,128)S(1)} %copy.89), channel_id=3, replica_groups=mesh['seq'=4,'tensor'=8] {'seq'}, dimensions={0}, use_global_device_ids=true | all-gather | bytes 5120 | tf_op jit(solution)/shard_map/all_gather | solution.py:19
  121.7 8.2 %all-gather = f32[8,4,2,16]{3,1,2,0:T(4,128)S(1)} all-gather(f32[2,4,2,16]{3,1,2,0:T(4,128)S(1)} %copy.88), channel_id=2, replica_groups=mesh['seq'=4,'tensor'=8] {'seq'}, dimensions={0}, use_global_device_ids=true | all-gather | bytes 5120 | tf_op jit(solution)/shard_map/all_gather | solution.py:19
  129.9 0.7 while.19
  129.9 0.2 fusion.79
  130.2 0.2 fusion.79
  130.4 0.2 fusion.79
  130.6 0.1 copy.104
  130.7 0.1 copy.97
  130.8 0.7 dynamic-slice_bitcast_fusion.1
  131.6 0.1 copy.96
  131.7 0.7 dynamic-slice_convert_fusion
  132.4 0.3 fusion.74
  132.9 0.2 fusion.33
  133.1 14.0 %all_gather.35 = bf16[64,2,512]{2,0,1:T(8,128)(2,1)S(1)} all-gather(bf16[8,2,512]{2,0,1:T(8,128)(2,1)S(1)} %reshape.569), channel_id=1, replica_groups=mesh['seq'=4,'tensor'=8] {'tensor'}, dimensions={0}, use_global_device_ids=true | all-gather | bytes 147456 | tf_op jit(solution)/shard_map/all_gather | solution.py:165
  147.1 2.7 %fusion.16 = f32[64,256]{1,0:T(8,128)} fusion(bf16[8,512,256]{2,1,0:T(8,128)(2,1)} %param.19, f32[64,2,8]{0,2,1:T(8,128)S(1)} %fusion.59, bf16[64,2,512]{2,0,1:T(8,128)(2,1)S(1)} %all_gather.35), kind=kOutput, calls=%fused_computation.26 | convolution fusion | flops 268943360 | bytes 2297856 | tf_op jit(solution)/shard_map/nkh,ehd->nked/dot_general | solution.py:163
  149.8 1.4 bitcast_select_fusion
  151.2 21.8 %reduce-scatter.2.cloned.1.call-done = f32[16,256]{1,0:T(8,128)} async-done(((f32[64,256]{1,0:T(8,128)}), f32[16,256]{1,0:T(8,128)}) %reduce-scatter.2.cloned.1.call-update) | async-done | bytes 16400 | tf_op jit(solution)/shard_map/reduce_scatter | solution.py:171
  173.0 1.4 broadcast_select_fusion
  (69 shorter events, 2.0 us)
Async XLA Ops:
  7.2 10.0 %copy-start = (bf16[8,256,512]{2,1,0:T(8,128)(2,1)S(1)}, bf16[8,256,512]{2,1,0:T(8,128)(2,1)}, u32[]{:S(2)}) copy-start(bf16[8,256,512]{2,1,0:T(8,128)(2,1)} %param.17) | copy-start | bytes 6291460
  7.2 15.2 %copy-start.5 = (s32[16]{0:T(128)S(1)}, s32[16]{0:T(128)}, u32[]{:S(2)}) copy-start(s32[16]{0:T(128)} %param.24) | copy-start | bytes 196
  7.2 15.4 %copy-start.6 = (s32[16]{0:T(128)S(1)}, s32[16]{0:T(128)}, u32[]{:S(2)}) copy-start(s32[16]{0:T(128)} %param.22) | copy-start | bytes 196
  7.2 71.5 %all-reduce.2.cloned.1.call-start = ((), (), s32[]{:S(2)}) async-start(), calls=%async_computation.1 | async-start | bytes 1048576 | tf_op jit(solution)/shard_map/psum | solution.py:88
  22.1 150.9 %reduce-scatter.2.cloned.1.call-start = ((), (), s32[]{:S(2)}) async-start(), calls=%async_computation.2 | async-start | bytes 81920 | tf_op jit(solution)/shard_map/reduce_scatter | solution.py:171
  69.1 8.1 %copy-start.3 = (s32[64,2]{0,1:T(2,128)S(1)}, s32[64,2]{0,1:T(2,128)}, u32[]{:S(2)}) copy-start(s32[64,2]{0,1:T(2,128)} %param.16) | copy-start | bytes 1540
  69.1 8.1 %copy-start.4 = (f32[64,8]{0,1:T(8,128)S(1)}, f32[64,8]{0,1:T(8,128)}, u32[]{:S(2)}) copy-start(f32[64,8]{0,1:T(8,128)} %param.15) | copy-start | bytes 6148
  69.1 8.2 %copy-start.2 = (s32[16]{0:T(128)S(1)}, s32[16]{0:T(128)}, u32[]{:S(2)}) copy-start(s32[16]{0:T(128)} %param.25) | copy-start | bytes 196
  95.9 78.5 %copy-start.1 = (bf16[8,256,512]{2,1,0:T(8,128)(2,1)S(1)}, bf16[8,256,512]{2,1,0:T(8,128)(2,1)}, u32[]{:S(2)}) copy-start(bf16[8,256,512]{2,1,0:T(8,128)(2,1)} %param.17) | copy-start | bytes 6291460
Sparse Core Ops, SparseCore 0:
  22.2 56.4 all-reduce.1
  149.9 23.0 reduce-scatter.1
where the time goes:
time: 182 us; the launch traced here: 181 us
  local copies, waits for them, and re-layouts  59.3 us (33%)
  blocking collectives  57.6 us (32%)
  waiting for transfers between devices  21.8 us (12%)
  matrix products  20.5 us (11%)
  between operations  14.3 us (8%)
  other arithmetic  7.4 us (4%)
    all_gather x3, blocking collectives, joined_2(): gathered = jax.tree.map(lambda a: lax.all_gather(a, axis), part)  25.4 us
    reduce_scatter x1, waiting for transfers between devices, per_device(): lax.psum_scatter(partial_out, 'seq', scatter_dimension=0, tiled=True)  21.8 us
    unnamed x16, local copies, waits for them, and re-layouts  19.6 us
    all_gather x1, blocking collectives, per_device(): lax.all_gather(attended, 'tensor', axis=0, tiled=True)  14 us
    all_gather x1, blocking collectives, per_device(): columns = lax.all_gather(hidden, 'seq', axis=0, tiled=True)  9.88 us
    gather x1, local copies, waits for them, and re-layouts, per_device(): cache_keys = k_cache[slots].reshape(req_own, key_count, kv_heads, HD)  8.44 us
    gather x1, local copies, waits for them, and re-layouts, per_device(): cache_values = v_cache[slots].reshape(req_own, key_count, kv_heads, HD)  8.41 us
    all_gather x1, blocking collectives, per_device(): queries_all = lax.all_gather(queries, 'seq', axis=2, tiled=True)  8.37 us
  transfers between devices with their start and end apart: 2, of which 1 were waited for; matrix products, arithmetic and copies ran while one was open for 32% of the time, Pallas kernels for 0%

commit v1 on v0

v1 whole, which is shorter than its diff:
```python
import functools
import math

import jax
import jax.numpy as jnp
from jax import lax
from jax.experimental import pallas as pl
from jax.experimental.pallas import tpu as pltpu
from jax.sharding import PartitionSpec as P

HD = 128
Q = 4
PAGE = 64
MAXP = 64
CHUNK = 4
TRANSFER = 8 * 2**30


THETA = 10000.0
NEGATIVE = -1e30
VMEM = pl.BlockSpec(memory_space=pltpu.VMEM)
SMEM = pl.BlockSpec(memory_space=pltpu.SMEM)
HBM = pl.BlockSpec(memory_space=pltpu.HBM)
ANY = pl.BlockSpec(memory_space=pl.ANY)


def call(
    body, out_shape, in_specs, *args, out_specs=None, scratch=(), flops=0, moved=0, limit=16
):
    single = not isinstance(out_shape, (list, tuple))
    if out_specs is None:
        out_specs = VMEM if single else [VMEM] * len(out_shape)
    return pl.pallas_call(
        body,
        out_shape=out_shape,
        in_specs=in_specs,
        out_specs=out_specs,
        scratch_shapes=list(scratch),
        compiler_params=pltpu.CompilerParams(vmem_limit_bytes=limit * 2**20),
        cost_estimate=pl.CostEstimate(flops=flops, bytes_accessed=moved, transcendentals=0),
    )(*args)


def in_hbm(array):
    return pltpu.with_memory_space_constraint(array, pltpu.HBM)


def offsets_of(size):
    return [0, *reversed(range(1, size))]


def swapped(blocks, axis, step=1):
    size = lax.axis_size(axis)
    return [
        lax.ppermute(block, axis, [(i, i ^ (d * step)) for i in range(size)]) if d else block
        for d, block in zip(offsets_of(len(blocks)), blocks)
    ]


def neighbour(block):
    size = lax.axis_size("tensor")
    return lax.ppermute(block, "tensor", [(i, i ^ 1) for i in range(size)])


def turned(vectors, cosine, sine):
    return vectors * cosine + pltpu.roll(vectors, HD // 2, 1) * sine


def column_of(row):
    size = row.shape[1]
    place = lax.broadcasted_iota(jnp.int32, (size, size), 0)
    other = lax.broadcasted_iota(jnp.int32, (size, size), 1)
    return jnp.sum(jnp.where(place == other, row, 0.0), axis=1, keepdims=True)


def table_kernel(
    seq_count,
    req_own,
    pages_here,
    routes_ref,
    accepted_ref,
    lengths_ref,
    table_ref,
    home_ref,
    tokens_ref,
    plan_ref,
    routes_buf,
    accepted_buf,
    lengths_buf,
    table_buf,
    home_buf,
    sem,
):
    sources = (routes_ref, accepted_ref, lengths_ref, table_ref, home_ref)
    targets = (routes_buf, accepted_buf, lengths_buf, table_buf, home_buf)
    copies = [
        pltpu.make_async_copy(source, target, sem.at[i])
        for i, (source, target) in enumerate(zip(sources, targets))
    ]
    for copy in copies:
        copy.start()
    for copy in copies:
        copy.wait()
    seq_index = lax.axis_index("seq")
    tensor_index = lax.axis_index("tensor")
    for r in range(req_own):
        request = tensor_index * req_own + r
        offset = (seq_index - home_buf[request] + seq_count) % seq_count
        length = lengths_buf[request]
        pages = ((length + PAGE - 1) // PAGE - offset + seq_count - 1) // seq_count
        plan_ref[r, 0] = (pages + CHUNK - 1) // CHUNK
        plan_ref[r, 1] = length
        plan_ref[r, 2] = offset
        for p in range(pages_here):
            plan_ref[r, 3 + p] = table_buf[request, offset + seq_count * p]
    tokens = tokens_ref.shape[0]
    requests = accepted_ref.shape[1]
    lane = lax.broadcasted_iota(jnp.int32, tokens_ref.shape, 1)
    table = jnp.zeros(tokens_ref.shape, jnp.float32)
    for k in range(2):
        column = column_of(routes_buf[k : k + 1, :].astype(jnp.float32))
        table = jnp.where(lane == k, column, table)
    row = lax.broadcasted_iota(jnp.int32, (tokens, requests), 0)
    request = lax.broadcasted_iota(jnp.int32, (tokens, requests), 1)
    limit = jnp.sum(
        jnp.where(row // Q == request, accepted_buf[...].astype(jnp.float32), 0.0),
        axis=1,
        keepdims=True,
    )
    step = (lax.broadcasted_iota(jnp.int32, (tokens, 1), 0) % Q).astype(jnp.float32)
    table = jnp.where(lane == 2, jnp.where(step < limit, 1.0, 0.0), table)
    tokens_ref[...] = table.astype(jnp.int32)


def project_kernel(seq_count, *refs):
    hidden_refs = refs[:seq_count]
    tokens_ref, query_weight_ref, keyval_weight_ref = refs[seq_count : seq_count + 3]
    keep_ref, give_ref, columns_ref = refs[seq_count + 3 :]
    seq_index = lax.axis_index("seq")
    rows = hidden_refs[0].shape[0]
    for d, hidden_ref in zip(offsets_of(seq_count), hidden_refs):
        start = pl.multiple_of((seq_index ^ d) * rows, rows)
        columns_ref[pl.ds(start, rows), :] = hidden_ref[...]
    columns = columns_ref[...]
    experts, depth, width = query_weight_ref.shape
    weights = query_weight_ref[...].reshape(experts * depth, width)
    masked = []
    for e in range(experts):
        masked.append(
            jnp.concatenate(
                [
                    columns
                    * jnp.where(tokens_ref[:, k : k + 1] == e, 1.0, 0.0).astype(jnp.bfloat16)
                    for k in range(2)
                ],
                axis=0,
            )
        )
    queries = jnp.dot(
        jnp.concatenate(masked, axis=1), weights, preferred_element_type=jnp.float32
    )
    tokens = columns.shape[0]
    parts = [queries[:tokens], queries[tokens:]]
    for c in range(2):
        parts.append(jnp.dot(columns, keyval_weight_ref[c], preferred_element_type=jnp.float32))
    own = keep_ref.shape[1] // 4
    parity = lax.axis_index("tensor") % 2
    for t in range(2 * keep_ref.shape[0]):
        span = slice(t * own, (t + 1) * own)
        block = jnp.concatenate([part[span] for part in parts], axis=0).astype(jnp.bfloat16)

        @pl.when(parity == t % 2)
        def _():
            keep_ref[t // 2] = block

        @pl.when(parity != t % 2)
        def _():
            give_ref[t // 2] = block


def pair_kernel(keep_ref, arrived_ref, *out_refs):
    place = lax.axis_index("tensor") // 2
    for d, out_ref in zip(offsets_of(len(out_refs)), out_refs):
        out_ref[...] = (
            keep_ref[place ^ d].astype(jnp.float32) + arrived_ref[place ^ d].astype(jnp.float32)
        ).astype(jnp.bfloat16)


def total_of(refs, rows=slice(None)):
    return functools.reduce(jnp.add, [ref[rows].astype(jnp.float32) for ref in refs])


def by_request(rows, own):
    return jnp.concatenate(
        [
            rows[k * own + r * Q : k * own + (r + 1) * Q]
            for r in range(own // Q)
            for k in range(2)
        ],
        axis=0,
    )


def by_choice(rows, own):
    return jnp.concatenate(
        [
            rows[(r * 2 + k) * Q : (r * 2 + k + 1) * Q]
            for k in range(2)
            for r in range(own // Q)
        ],
        axis=0,
    )


def turn_kernel(cosine_ref, sine_ref, *refs):
    parts, out_ref = refs[:-1], refs[-1]
    own = out_ref.shape[0] // 2
    total = total_of(parts, slice(0, 2 * own))
    cosine = jnp.concatenate([cosine_ref[...]] * 2, axis=0)
    sine = jnp.concatenate([sine_ref[...]] * 2, axis=0)
    heads = [
        turned(total[:, h * HD : (h + 1) * HD], cosine, sine) for h in range(total.shape[1] // HD)
    ]
    out_ref[...] = by_request(jnp.concatenate(heads, axis=1), own).astype(jnp.bfloat16)


def fresh_kernel(tokens_ref, cosine_ref, sine_ref, query_ref, *refs):
    parts, (keys_ref, values_ref, out_ref) = refs[:-3], refs[-3:]
    tensor_index = lax.axis_index("tensor")
    own = keys_ref.shape[0]
    total = total_of(parts, slice(2 * own, 4 * own))
    heads_here = total.shape[1] // HD
    keys = jnp.concatenate(
        [
            turned(total[:own, h * HD : (h + 1) * HD], cosine_ref[...], sine_ref[...])
            for h in range(heads_here)
        ],
        axis=1,
    )
    values = total[own:]
    start = pl.multiple_of(tensor_index * own, own)
    kept = tokens_ref[pl.ds(start, own), 2:3] > 0
    keys_ref[...] = jnp.where(kept, keys, 0.0)
    values_ref[...] = jnp.where(kept, values, 0.0)
    rows = 2 * own
    query_row = lax.broadcasted_iota(jnp.int32, (rows, own), 0)
    key_row = lax.broadcasted_iota(jnp.int32, (rows, own), 1)
    valid = (query_row // (2 * Q) == key_row // Q) & (query_row % Q >= key_row % Q)
    lane = lax.broadcasted_iota(jnp.int32, (rows, HD), 1)
    notes = jnp.zeros((rows, HD), jnp.float32)
    for h in range(heads_here):
        span = slice(h * HD, (h + 1) * HD)
        scores = lax.dot_general(
            query_ref[:, span],
            keys[:, span].astype(jnp.bfloat16),
            (((1,), (1,)), ((), ())),
            preferred_element_type=jnp.float32,
        ) * (1.0 / math.sqrt(HD))
        scores = jnp.where(valid, scores, NEGATIVE)
        top = jnp.max(scores, axis=1, keepdims=True)
        weights = jnp.where(valid, jnp.exp(scores - top), 0.0)
        sums = jnp.sum(weights, axis=1, keepdims=True)
        mixed = jnp.dot(
            weights.astype(jnp.bfloat16),
            values[:, span].astype(jnp.bfloat16),
            preferred_element_type=jnp.float32,
        )
        out_ref[:, span] = mixed / sums
        notes = jnp.where(lane == h, top + jnp.log(sums), notes)
    out_ref[:, heads_here * HD :] = notes


def cache_kernel(seq_count, req_own, pages_here, plan_ref, *refs):
    query_refs = refs[:seq_count]
    k_buf, v_buf = refs[seq_count : seq_count + 2]
    out_refs = refs[seq_count + 2 : 2 * seq_count + 2]
    query_buf, spread, total_buf, out_buf = refs[2 * seq_count + 2 :]
    seq_index = lax.axis_index("seq")
    width = query_refs[0].shape[1]
    heads_here = width // HD
    kv_heads = heads_here * seq_count
    full = kv_heads * HD
    rows = 2 * Q
    lanes = kv_heads * rows
    chunk_keys = CHUNK * PAGE
    counts = [plan_ref[r, 0] for r in range(req_own)]
    lengths = [plan_ref[r, 1] for r in range(req_own)]
    offsets = [plan_ref[r, 2] for r in range(req_own)]
    for d, query_ref in zip(offsets_of(seq_count), query_refs):
        start = pl.multiple_of((seq_index ^ d) * width, width)
        query_buf[:, pl.ds(start, width)] = query_ref[...].astype(jnp.float32)
    row_head = lax.broadcasted_iota(jnp.int32, (lanes, full), 0) // rows
    column_head = lax.broadcasted_iota(jnp.int32, (lanes, full), 1) // HD
    diagonal = row_head == column_head
    for r in range(req_own):
        wide = jnp.concatenate([query_buf[r * rows : (r + 1) * rows, :full]] * kv_heads, axis=0)
        spread[r] = jnp.where(diagonal, wide, 0.0).T.astype(jnp.bfloat16)

    key_page = lax.broadcasted_iota(jnp.int32, (chunk_keys, lanes), 0) // PAGE
    key_row = lax.broadcasted_iota(jnp.int32, (chunk_keys, lanes), 0) % PAGE
    key_place = key_page * (seq_count * PAGE) + key_row
    for r in range(req_own):

        for count in range(pages_here // CHUNK + 1):

            @pl.when(counts[r] == count)
            def _():
                pairs = full // (2 * HD)
                if count == 0:
                    out_buf[...] = jnp.zeros_like(out_buf)
                    total_buf[...] = jnp.zeros_like(total_buf)
                    return
                slots = [plan_ref[r, 3 + p] for p in range(count * CHUNK)]
                scores = []
                for c in range(count):
                    keys = jnp.concatenate(
                        [k_buf[slot] for slot in slots[c * CHUNK : (c + 1) * CHUNK]], axis=0
                    )
                    score = jnp.dot(keys, spread[r], preferred_element_type=jnp.float32) * (
                        1.0 / math.sqrt(HD)
                    )
                    base = (offsets[r] + seq_count * CHUNK * c) * PAGE
                    scores.append(jnp.where(key_place < lengths[r] - base, score, NEGATIVE))
                top = functools.reduce(
                    jnp.maximum, [jnp.max(score, axis=0, keepdims=True) for score in scores]
                )
                weights = [jnp.exp(score - top) for score in scores]
                total_buf[0:1, :] = top
                total_buf[1:2, :] = functools.reduce(
                    jnp.add, [jnp.sum(weight, axis=0, keepdims=True) for weight in weights]
                )
                flipped = jnp.concatenate(
                    [weight.T.astype(jnp.bfloat16) for weight in weights], axis=1
                )
                for i in range(pairs):
                    span = slice(i * 2 * HD, (i + 1) * 2 * HD)
                    values = jnp.concatenate([v_buf[slot, :, span] for slot in slots], axis=0)
                    out_buf[:, span] = jnp.dot(
                        flipped[i * 2 * rows : (i + 1) * 2 * rows, :],
                        values,
                        preferred_element_type=jnp.float32,
                    )

        top, sums = total_buf[0:1, :], total_buf[1:2, :]
        some = sums > 0.0
        safe = jnp.where(some, sums, 1.0)
        logs = jnp.where(some, top + jnp.log(safe), NEGATIVE)
        inverse = jnp.broadcast_to(1.0 / safe, (HD, lanes)).T
        logs = jnp.broadcast_to(logs, (HD, lanes)).T
        lane = lax.broadcasted_iota(jnp.int32, (rows, HD), 1)
        for g in range(seq_count):
            notes = jnp.zeros((rows, HD), jnp.float32)
            for j in range(heads_here):
                h = g * heads_here + j
                half = (h % 2) * rows
                spread_rows = slice(h * rows, (h + 1) * rows)
                mixed = out_buf[half : half + rows, h * HD : (h + 1) * HD] * inverse[spread_rows]
                query_buf[r * rows : (r + 1) * rows, h * HD : (h + 1) * HD] = mixed
                log = logs[spread_rows]
                high = log.astype(jnp.bfloat16).astype(jnp.float32)
                middle = (log - high).astype(jnp.bfloat16).astype(jnp.float32)
                for part, value in enumerate((high, middle, log - high - middle)):
                    notes = jnp.where(lane == part * heads_here + j, value, notes)
            query_buf[r * rows : (r + 1) * rows, full + g * HD : full + (g + 1) * HD] = notes
    for d, out_ref in zip(offsets_of(seq_count), out_refs):
        group = seq_index ^ d
        start = pl.multiple_of(group * width, width)
        out_ref[:, :width] = query_buf[:, pl.ds(start, width)].astype(jnp.bfloat16)
        start = pl.multiple_of(full + group * HD, HD)
        out_ref[:, width:] = query_buf[:, pl.ds(start, HD)].astype(jnp.bfloat16)


def join_kernel(fresh_ref, *refs):
    parts, out_ref = refs[:-1], refs[-1]
    rows = fresh_ref.shape[0]
    own = rows // 2
    width = out_ref.shape[1]
    heads_here = width // HD
    fresh_notes = fresh_ref[:, width:]
    notes = [part[:, width:].astype(jnp.float32) for part in parts]
    heads = []
    for h in range(heads_here):
        span = slice(h * HD, (h + 1) * HD)
        logs = [fresh_notes[:, h : h + 1]]
        for note in notes:
            logs.append(
                note[:, h : h + 1]
                + note[:, heads_here + h : heads_here + h + 1]
                + note[:, 2 * heads_here + h : 2 * heads_here + h + 1]
            )
        top = functools.reduce(jnp.maximum, logs)
        shares = [jnp.exp(log - top) for log in logs]
        mixed = shares[0] * fresh_ref[:, span]
        for share, part in zip(shares[1:], parts):
            mixed = mixed + share * part[:, span].astype(jnp.float32)
        heads.append(mixed / functools.reduce(jnp.add, shares))
    out_ref[...] = by_choice(jnp.concatenate(heads, axis=1), own).astype(jnp.bfloat16)


def output_kernel(seq_count, tensor_count, tokens_ref, logits_ref, weight_ref, *refs):
    parts = refs[:tensor_count]
    out_refs = refs[tensor_count : tensor_count + seq_count]
    rows_ref, sum_ref = refs[tensor_count + seq_count :]
    seq_index = lax.axis_index("seq")
    tensor_index = lax.axis_index("tensor")
    rows = parts[0].shape[0]
    own = rows // 2
    pairs = [2 * d + half for d in offsets_of(tensor_count // 2) for half in range(2)]
    for d, part in zip(pairs, parts):
        start = pl.multiple_of((tensor_index ^ d) * rows, rows)
        rows_ref[pl.ds(start, rows), :] = part[...]
    experts = weight_ref.shape[0]
    routes = [tokens_ref[:, k : k + 1] for k in range(2)]
    column = lax.broadcasted_iota(jnp.int32, logits_ref.shape, 1)
    logits = logits_ref[...]
    chosen = [
        jnp.sum(jnp.where(column == route, logits, 0.0), axis=1, keepdims=True) for route in routes
    ]
    top = jnp.maximum(chosen[0], chosen[1])
    grown = [jnp.exp(value - top) for value in chosen]
    kept = tokens_ref[:, 2:3] > 0
    gates = [jnp.where(kept, value / (grown[0] + grown[1]), 0.0) for value in grown]
    row_route = jnp.concatenate(
        [routes[k][t * own : (t + 1) * own] for t in range(tensor_count) for k in range(2)], axis=0
    )
    attended = rows_ref[...]
    total = None
    for e in range(experts):
        masked = attended * jnp.where(row_route == e, 1.0, 0.0).astype(jnp.bfloat16)
        product = jnp.dot(masked, weight_ref[e], preferred_element_type=jnp.float32)
        total = product if total is None else total + product
    for t in range(tensor_count):
        span = slice(t * own, (t + 1) * own)
        sum_ref[span, :] = (
            gates[0][span] * total[t * rows : t * rows + own]
            + gates[1][span] * total[t * rows + own : (t + 1) * rows]
        )
    height = out_refs[0].shape[0]
    for d, out_ref in zip(offsets_of(seq_count), out_refs):
        start = pl.multiple_of((seq_index ^ d) * height, height)
        out_ref[...] = sum_ref[pl.ds(start, height), :].astype(out_ref.dtype)


def add_kernel(*refs):
    refs[-1][...] = total_of(refs[:-1])


def per_device(
    hidden,
    router_logits,
    routes,
    w_query,
    w_keyval,
    w_output,
    k_cache,
    v_cache,
    lengths,
    page_table,
    home_device,
    accepted,
):
    seq_count = lax.axis_size("seq")
    tensor_count = lax.axis_size("tensor")
    tok_total = routes.shape[0]
    tok_own = tok_total // tensor_count
    req_own = tok_own // Q
    experts, depth, width = w_query.shape
    out_width = w_output.shape[2]
    heads_here = width // HD
    kv_heads = heads_here * seq_count
    full = kv_heads * HD
    pages_here = MAXP // seq_count
    rows = 2 * tok_own
    height = tok_total // seq_count
    bf16, f32 = jnp.bfloat16, jnp.float32

    def shape(dims, dtype):
        return jax.ShapeDtypeStruct(dims, dtype)

    with jax.named_scope("gather_hidden"):
        hiddens = swapped([hidden] * seq_count, "seq")
    with jax.named_scope("make_tables"):
        tokens, plan = call(
            functools.partial(table_kernel, seq_count, req_own, pages_here),
            [
                shape((tok_total, HD), jnp.int32),
                shape((req_own, 3 + pages_here), jnp.int32),
            ],
            [HBM] * 5,
            in_hbm(routes.T),
            in_hbm(accepted.reshape(1, -1)),
            in_hbm(lengths),
            in_hbm(page_table),
            in_hbm(home_device),
            out_specs=[VMEM, SMEM],
            scratch=[
                pltpu.VMEM((2, tok_total), jnp.int32),
                pltpu.VMEM((1, accepted.shape[0]), jnp.int32),
                pltpu.SMEM(lengths.shape, jnp.int32),
                pltpu.SMEM(page_table.shape, jnp.int32),
                pltpu.SMEM(home_device.shape, jnp.int32),
                pltpu.SemaphoreType.DMA((5,)),
            ],
            flops=TRANSFER,
        )
        keyval_weight = jnp.swapaxes(w_keyval, 0, 1)
    with jax.named_scope("project_tokens"):
        half = shape((tensor_count // 2, 2 * rows, width), bf16)
        keep, give = call(
            functools.partial(project_kernel, seq_count),
            [half] * 2,
            [VMEM] * (seq_count + 3),
            *hiddens,
            tokens,
            w_query,
            keyval_weight,
            scratch=[pltpu.VMEM((tok_total, depth), bf16)],
            flops=2 * TRANSFER,
        )
    with jax.named_scope("sum_tokens"):
        parts = call(
            pair_kernel,
            [shape((2 * rows, width), bf16)] * (tensor_count // 2),
            [VMEM] * 2,
            keep,
            neighbour(give),
        )
        parts = swapped(parts, "tensor", 2)
    with jax.named_scope("rotation_table"):
        positions = jnp.repeat(plan[:, 1], Q) + jnp.arange(tok_own, dtype=jnp.int32) % Q
        inverse = THETA ** (-(jnp.arange(HD // 2, dtype=f32) * 2.0 / HD))
        angles = positions.astype(f32)[:, None] * inverse
        cosine = jnp.cos(angles)
        sine = jnp.sin(angles)
        cosine = jnp.concatenate([cosine, cosine], axis=1)
        sine = jnp.concatenate([-sine, sine], axis=1)
    with jax.named_scope("rotate_queries"):
        queries = call(
            turn_kernel,
            shape((rows, width), bf16),
            [VMEM] * (2 + tensor_count // 2),
            cosine,
            sine,
            *parts,
        )
    with jax.named_scope("gather_queries"):
        queries_all = swapped([queries] * seq_count, "seq")
    with jax.named_scope("attend_fresh"):
        new_keys, new_values, fresh = call(
            fresh_kernel,
            [shape((tok_own, width), f32)] * 2 + [shape((rows, width + HD), f32)],
            [VMEM] * (4 + tensor_count // 2),
            tokens,
            cosine,
            sine,
            queries,
            *parts,
            moved=rows * width * 2 * tensor_count,
        )
    with jax.named_scope("attend_cache"):
        cache_parts = call(
            functools.partial(cache_kernel, seq_count, req_own, pages_here),
            [shape((rows, width + HD), bf16)] * seq_count,
            [SMEM] + [VMEM] * (seq_count + 2),
            plan,
            *queries_all,
            k_cache,
            v_cache,
            scratch=[
                pltpu.VMEM((rows, full + seq_count * HD), f32),
                pltpu.VMEM((req_own, full, kv_heads * 2 * Q), bf16),
                pltpu.VMEM((8, kv_heads * 2 * Q), f32),
                pltpu.VMEM((4 * Q, full), f32),
            ],
            flops=4 * req_own * pages_here * PAGE * full * kv_heads * 2 * Q,
            moved=req_own * pages_here * PAGE * full * 4,
            limit=28,
        )
    with jax.named_scope("trade_partials"):
        cache_parts = swapped(cache_parts, "seq")
    with jax.named_scope("join_partials"):
        attended = call(
            join_kernel,
            shape((rows, width), bf16),
            [VMEM] * (1 + seq_count),
            fresh,
            *cache_parts,
            moved=rows * width * 2 * seq_count,
        )
    with jax.named_scope("gather_attended"):
        far = swapped([attended] * (tensor_count // 2), "tensor", 2)
        attended_all = [part for block in far for part in (block, neighbour(block))]
    with jax.named_scope("project_output"):
        out_parts = call(
            functools.partial(output_kernel, seq_count, tensor_count),
            [shape((height, out_width), bf16)] * seq_count,
            [VMEM] * (3 + tensor_count),
            tokens,
            router_logits,
            w_output,
            *attended_all,
            scratch=[
                pltpu.VMEM((tensor_count * rows, width), bf16),
                pltpu.VMEM((tok_total, out_width), f32),
            ],
            flops=4 * tok_total * experts * width * out_width,
            moved=w_output.size * 2,
        )
    with jax.named_scope("sum_output"):
        out_parts = swapped(out_parts, "seq")
    with jax.named_scope("add_output"):
        attn_out = call(
            add_kernel,
            shape((height, out_width), f32),
            [VMEM] * seq_count,
            *out_parts,
            moved=height * out_width * 2 * seq_count,
        )
    return (attn_out, new_keys, new_values)


def solution(mesh):
    in_specs = (
        P("seq", "tensor"),
        P(),
        P(),
        P(None, "tensor", "seq"),
        P("tensor", None, "seq"),
        P(None, "seq", "tensor"),
        P(("seq", "tensor"), None, None),
        P(("seq", "tensor"), None, None),
        P(),
        P(),
        P(),
        P(),
    )
    out_specs = (P("seq", "tensor"), P("tensor", "seq"), P("tensor", "seq"))
    return jax.shard_map(
        per_device, mesh=mesh, in_specs=in_specs, out_specs=out_specs, check_vma=False
    )
```

time: 182 us -> 50.4 us (0.28)
  local copies, waits for them, and re-layouts: 59.3 us -> 0.52 us
  blocking collectives: 57.6 us -> 0 us
  starting transfers between devices: 0.26 us -> 24.6 us
  matrix products: 20.5 us -> 0 us
  between operations: 14.3 us -> 0.8 us
  Pallas kernels: 0 us -> 8.09 us
  other arithmetic: 7.4 us -> 0.2 us
  waiting for transfers between devices: 21.8 us -> 15.7 us
    all_gather x6 -> x0, blocking collectives: 57.6 us -> none  [the longest x3 25.4 us: joined_2(): gathered = jax.tree.map(lambda a: lax.all_gather(a, axis), part)]
    ppermute x0 -> x23, starting transfers between devices: none -> 24.6 us  [the longest x18 24.2 us: swapped(): lax.ppermute(block, axis, [(i, i ^ d * step) for i in range(size)])]
    reduce_scatter x1 -> x0, waiting for transfers between devices: 21.8 us -> none  [per_device(): lax.psum_scatter(partial_out, 'seq', scatter_dimension=0, tiled=True)]
    dot_general x7 -> x0, matrix products: 20.5 us -> none  [the longest x1 7.77 us: per_device(): jnp.einsum('rqkhl,rlhd->rqkhd', weights.astype(jnp.bfloat16), cache_value...]
    unnamed x16 -> x20, local copies, waits for them, and re-layouts: 19.6 us -> 0.18 us
    gather x6 -> x0, local copies, waits for them, and re-layouts: 18.4 us -> none  [the longest x1 8.44 us: per_device(): cache_keys = k_cache[slots].reshape(req_own, key_count, kv_heads, HD)]
    reshape x6 -> x1, local copies, waits for them, and re-layouts: 17.1 us -> 0.08 us  [per_device(): jnp.repeat(plan[:, 1], Q) + jnp.arange(tok_own, dtype=jnp.int32) % Q]
    ppermute x0 -> x23, waiting for transfers between devices: none -> 15.7 us  [the longest x18 13.3 us: swapped(): lax.ppermute(block, axis, [(i, i ^ d * step) for i in range(size)])]
  transfers between devices with their start and end apart: 2 -> 23, of which waited for: 1 -> 20; matrix products, arithmetic and copies ran while one was open for 32% -> 1% of each run, Pallas kernels for 0% -> 6%
where the time goes in v1:
time: 50.4 us; the launch traced here: 49.9 us
  starting transfers between devices  24.6 us (49%)
  waiting for transfers between devices  15.7 us (31%)
  Pallas kernels  8.09 us (16%)
  between operations  0.8 us (2%)
  local copies, waits for them, and re-layouts  0.52 us (1%)
    ppermute x18, starting transfers between devices, swapped(): lax.ppermute(block, axis, [(i, i ^ d * step) for i in range(size)])  24.2 us
    ppermute x18, waiting for transfers between devices, swapped(): lax.ppermute(block, axis, [(i, i ^ d * step) for i in range(size)])  13.3 us
    pallas_call x9, Pallas kernels, call(): pl.pallas_call(body, out_shape=out_shape, in_specs=in_specs, out_specs=ou...  8.09 us
    ppermute x5, waiting for transfers between devices, neighbour(): return lax.ppermute(block, 'tensor', [(i, i ^ 1) for i in range(size)])  2.32 us
  transfers between devices with their start and end apart: 23, of which 20 were waited for; matrix products, arithmetic and copies ran while one was open for 1% of the time, Pallas kernels for 6%

profile of v1, /device:TPU:0, one launch (start us, length us, event | category | flops | bytes accessed | tf_op | source)
XLA Modules:
  0.0 49.9 jit_solution(12862254758294921826)
XLA Ops:
  0.6 4.0 %collective-permute-start = (bf16[16,256]{1,0:T(8,128)(2,1)}, bf16[16,256]{1,0:T(8,128)(2,1)S(1)}, u32[]{:S(2)}, u32[]{:S(2)}) collective-permute-start(bf16[16,256]{1,0:T(8,128)(2,1)} %refs_0_.1), channel_id=1, source_target_pairs={{0,24},{8,16},{16,8},{24,0},{1,25},{9,17},{17,9},{25,1},{2,26},{10... | collective-permute-start | bytes 24584 | tf_op jit(solution)/shard_map/gather_hidden/ppermute | solution.py:55
  4.6 0.5 %collective-permute-start.1 = (bf16[16,256]{1,0:T(8,128)(2,1)}, bf16[16,256]{1,0:T(8,128)(2,1)S(1)}, u32[]{:S(2)}, u32[]{:S(2)}) collective-permute-start(bf16[16,256]{1,0:T(8,128)(2,1)} %refs_0_.1), channel_id=1, source_target_pairs={{0,16},{8,24},{16,0},{24,8},{1,17},{9,25},{17,1},{25,9},{2,18},{10... | collective-permute-start | bytes 24584 | tf_op jit(solution)/shard_map/gather_hidden/ppermute | solution.py:55
  5.1 0.1 collective-permute-start.2
  5.2 1.7 %make_tables.1 = (s32[64,128]{1,0:T(8,128)S(1)}, s32[2,19]{1,0:T(2,128)S(1)}) custom-call(s32[2,64]{1,0:T(2,128)} %bitcast.10, s32[1,16]{1,0:T(1,128)} %bitcast.11, s32[16]{0:T(128)} %lengths_ref.1, s32[16,64]{1,0:T(8,128)} %table_ref.1, s32[16]{0:T(128)} %home_ref.1), custom_call_target="tpu_custom_call" | custom-call | flops 8589934592 | tf_op jit(solution)/shard_map/make_tables/pallas_call | solution.py:33
  6.9 0.2 slice_reduce_fusion
  7.4 1.0 %collective-permute-done.1.refs_2_ = bf16[16,256]{1,0:T(8,128)(2,1)S(1)} collective-permute-done((bf16[16,256]{1,0:T(8,128)(2,1)}, bf16[16,256]{1,0:T(8,128)(2,1)S(1)}, u32[]{:S(2)}, u32[]{:S(2)}) %collective-permute-start.1) | collective-permute-done | bytes 8224 | tf_op jit(solution)/shard_map/gather_hidden/ppermute | solution.py:55
  8.5 0.5 %collective-permute-done.2.refs_3_ = bf16[16,256]{1,0:T(8,128)(2,1)S(1)} collective-permute-done((bf16[16,256]{1,0:T(8,128)(2,1)}, bf16[16,256]{1,0:T(8,128)(2,1)S(1)}, u32[]{:S(2)}, u32[]{:S(2)}) %collective-permute-start.2) | collective-permute-done | bytes 8224 | tf_op jit(solution)/shard_map/gather_hidden/ppermute | solution.py:55
  9.0 0.6 %project_tokens.1 = (bf16[4,32,512]{2,1,0:T(8,128)(2,1)S(1)}, bf16[4,32,512]{2,1,0:T(8,128)(2,1)S(1)}) custom-call(bf16[16,256]{1,0:T(8,128)(2,1)S(1)} %copy-done.2, bf16[16,256]{1,0:T(8,128)(2,1)S(1)} %collective-permute-done.refs_1_, bf16[16,256]{1,0:T(8,128)(2,1)S(1)} %collective-permute-done.1.refs_2_, ...), custom_call_target="tpu_custom_call" | custom-call | flops 17179869184 | tf_op jit(solution)/shard_map/project_tokens/pallas_call | solution.py:33
  9.7 0.1 fusion
  9.8 1.2 %collective-permute-done.3.arrived_ref = bf16[4,32,512]{2,1,0:T(8,128)(2,1)S(1)} collective-permute-done((bf16[4,32,512]{2,1,0:T(8,128)(2,1)S(1)}, bf16[4,32,512]{2,1,0:T(8,128)(2,1)S(1)}, u32[]{:S(2)}, u32[]{:S(2)}) %collective-permute-start.3) | collective-permute-done | bytes 131104 | tf_op jit(solution)/shard_map/sum_tokens/ppermute | solution.py:62
  11.0 3.7 %collective-permute-start.4 = (bf16[32,512]{1,0:T(8,128)(2,1)S(1)}, bf16[32,512]{1,0:T(8,128)(2,1)S(1)}, u32[]{:S(2)}, u32[]{:S(2)}) collective-permute-start(bf16[32,512]{1,0:T(8,128)(2,1)S(1)} %get-tuple-element.27), channel_id=1, source_target_pairs={{0,6},{1,7},{2,4},{3,5},{4,2},{5,3},{6,0},{7,1},{8,14},{9,15},{10,... | collective-permute-start | bytes 98312 | tf_op jit(solution)/shard_map/sum_tokens/ppermute | solution.py:55
  14.7 0.8 %collective-permute-start.6 = (bf16[32,512]{1,0:T(8,128)(2,1)S(1)}, bf16[32,512]{1,0:T(8,128)(2,1)S(1)}, u32[]{:S(2)}, u32[]{:S(2)}) collective-permute-start(bf16[32,512]{1,0:T(8,128)(2,1)S(1)} %get-tuple-element.29), channel_id=1, source_target_pairs={{0,2},{1,3},{2,0},{3,1},{4,6},{5,7},{6,4},{7,5},{8,10},{9,11},{10,... | collective-permute-start | bytes 98312 | tf_op jit(solution)/shard_map/sum_tokens/ppermute | solution.py:55
  15.6 1.2 %collective-permute-done.4.refs_1_ = bf16[32,512]{1,0:T(8,128)(2,1)S(1)} collective-permute-done((bf16[32,512]{1,0:T(8,128)(2,1)S(1)}, bf16[32,512]{1,0:T(8,128)(2,1)S(1)}, u32[]{:S(2)}, u32[]{:S(2)}) %collective-permute-start.4) | collective-permute-done | bytes 32800 | tf_op jit(solution)/shard_map/sum_tokens/ppermute | solution.py:55
  16.8 2.7 %collective-permute-done.5.refs_2_ = bf16[32,512]{1,0:T(8,128)(2,1)S(1)} collective-permute-done((bf16[32,512]{1,0:T(8,128)(2,1)S(1)}, bf16[32,512]{1,0:T(8,128)(2,1)S(1)}, u32[]{:S(2)}, u32[]{:S(2)}) %collective-permute-start.5) | collective-permute-done | bytes 32800 | tf_op jit(solution)/shard_map/sum_tokens/ppermute | solution.py:55
  19.5 0.1 rotate_queries.1.query_ref.refs_0_
  19.6 1.6 %collective-permute-start.7 = (bf16[16,512]{1,0:T(8,128)(2,1)S(1)}, bf16[16,512]{1,0:T(8,128)(2,1)S(1)}, u32[]{:S(2)}, u32[]{:S(2)}) collective-permute-start(bf16[16,512]{1,0:T(8,128)(2,1)S(1)} %rotate_queries.1.query_ref.refs_0_), channel_id=1, source_target_pairs={{0,24},{8,16},{16,8},{24,0},{1,25},{9,17},{17,9},{25,1},{2,26},{10... | collective-permute-start | bytes 49160 | tf_op jit(solution)/shard_map/gather_queries/ppermute | solution.py:55
  21.2 0.5 %collective-permute-start.8 = (bf16[16,512]{1,0:T(8,128)(2,1)S(1)}, bf16[16,512]{1,0:T(8,128)(2,1)S(1)}, u32[]{:S(2)}, u32[]{:S(2)}) collective-permute-start(bf16[16,512]{1,0:T(8,128)(2,1)S(1)} %rotate_queries.1.query_ref.refs_0_), channel_id=1, source_target_pairs={{0,16},{8,24},{16,0},{24,8},{1,17},{9,25},{17,1},{25,9},{2,18},{10... | collective-permute-start | bytes 49160 | tf_op jit(solution)/shard_map/gather_queries/ppermute | solution.py:55
  21.7 1.5 %collective-permute-start.9 = (bf16[16,512]{1,0:T(8,128)(2,1)S(1)}, bf16[16,512]{1,0:T(8,128)(2,1)S(1)}, u32[]{:S(2)}, u32[]{:S(2)}) collective-permute-start(bf16[16,512]{1,0:T(8,128)(2,1)S(1)} %rotate_queries.1.query_ref.refs_0_), channel_id=1, source_target_pairs={{0,8},{8,0},{16,24},{24,16},{1,9},{9,1},{17,25},{25,17},{2,10},{10... | collective-permute-start | bytes 49160 | tf_op jit(solution)/shard_map/gather_queries/ppermute | solution.py:55
  23.2 1.1 %collective-permute-done.7.refs_1_ = bf16[16,512]{1,0:T(8,128)(2,1)S(1)} collective-permute-done((bf16[16,512]{1,0:T(8,128)(2,1)S(1)}, bf16[16,512]{1,0:T(8,128)(2,1)S(1)}, u32[]{:S(2)}, u32[]{:S(2)}) %collective-permute-start.7) | collective-permute-done | bytes 16416 | tf_op jit(solution)/shard_map/gather_queries/ppermute | solution.py:55
  24.3 0.6 %collective-permute-done.8.refs_2_ = bf16[16,512]{1,0:T(8,128)(2,1)S(1)} collective-permute-done((bf16[16,512]{1,0:T(8,128)(2,1)S(1)}, bf16[16,512]{1,0:T(8,128)(2,1)S(1)}, u32[]{:S(2)}, u32[]{:S(2)}) %collective-permute-start.8) | collective-permute-done | bytes 16416 | tf_op jit(solution)/shard_map/gather_queries/ppermute | solution.py:55
  24.9 0.5 %collective-permute-done.9.refs_3_ = bf16[16,512]{1,0:T(8,128)(2,1)S(1)} collective-permute-done((bf16[16,512]{1,0:T(8,128)(2,1)S(1)}, bf16[16,512]{1,0:T(8,128)(2,1)S(1)}, u32[]{:S(2)}, u32[]{:S(2)}) %collective-permute-start.9) | collective-permute-done | bytes 16416 | tf_op jit(solution)/shard_map/gather_queries/ppermute | solution.py:55
  25.5 3.1 %attend_cache.1 = (bf16[16,640]{1,0:T(8,128)(2,1)S(1)}, bf16[16,640]{1,0:T(8,128)(2,1)S(1)}, bf16[16,640]{1,0:T(8,128)(2,1)S(1)}, bf16[16,640]{1,0:T(8,128)(2,1)S(1)}) custom-call(s32[2,19]{1,0:T(2,128)S(1)} %get-tuple-element.23.plan_ref, bf16[16,512]{1,0:T(8,128)(2,1)S(1)} %rotate_queries.1.query_ref.refs_0_, ...), custom_call_target="tpu_custom_call" | custom-call | flops 2147483648 | bytes 16777216 | tf_op jit(solution)/shard_map/attend_cache/pallas_call | solution.py:33
  28.6 2.5 %collective-permute-start.10 = (bf16[16,640]{1,0:T(8,128)(2,1)S(1)}, bf16[16,640]{1,0:T(8,128)(2,1)S(1)}, u32[]{:S(2)}, u32[]{:S(2)}) collective-permute-start(bf16[16,640]{1,0:T(8,128)(2,1)S(1)} %get-tuple-element.32), channel_id=1, source_target_pairs={{0,24},{8,16},{16,8},{24,0},{1,25},{9,17},{17,9},{25,1},{2,26},{10... | collective-permute-start | bytes 61448 | tf_op jit(solution)/shard_map/trade_partials/ppermute | solution.py:55
  31.1 0.5 collective-permute-start.11
  31.6 0.5 %collective-permute-start.12 = (bf16[16,640]{1,0:T(8,128)(2,1)S(1)}, bf16[16,640]{1,0:T(8,128)(2,1)S(1)}, u32[]{:S(2)}, u32[]{:S(2)}) collective-permute-start(bf16[16,640]{1,0:T(8,128)(2,1)S(1)} %get-tuple-element.34), channel_id=1, source_target_pairs={{0,8},{8,0},{16,24},{24,16},{1,9},{9,1},{17,25},{25,17},{2,10},{10... | collective-permute-start | bytes 61448 | tf_op jit(solution)/shard_map/trade_partials/ppermute | solution.py:55
  32.1 1.2 %attend_fresh.1 = (f32[8,512]{1,0:T(8,128)}, f32[8,512]{1,0:T(8,128)}, f32[16,640]{1,0:T(8,128)S(1)}) custom-call(s32[64,128]{1,0:T(8,128)S(1)} %get-tuple-element.22.refs_4_.tokens_ref, f32[8,128]{1,0:T(8,128)S(1)} %get-tuple-element.44.cosine_ref, f32[8,128]{1,0:T(8,128)S(1)} %get-tuple-element.45.sine_ref, ...), custom_call_target="tpu_custom_call" | custom-call | bytes 131072 | tf_op jit(solution)/shard_map/attend_fresh/pallas_call | solution.py:33
  33.3 0.2 collective-permute-done.10.refs_1_
  33.5 1.4 %collective-permute-done.11.refs_2_ = bf16[16,640]{1,0:T(8,128)(2,1)S(1)} collective-permute-done((bf16[16,640]{1,0:T(8,128)(2,1)S(1)}, bf16[16,640]{1,0:T(8,128)(2,1)S(1)}, u32[]{:S(2)}, u32[]{:S(2)}) %collective-permute-start.11) | collective-permute-done | bytes 20512 | tf_op jit(solution)/shard_map/trade_partials/ppermute | solution.py:55
  34.9 0.5 collective-permute-done.12.refs_3_
  35.4 0.2 join_partials.1.refs_0_
  35.6 1.1 %collective-permute-start.14 = (bf16[16,512]{1,0:T(8,128)(2,1)S(1)}, bf16[16,512]{1,0:T(8,128)(2,1)S(1)}, u32[]{:S(2)}, u32[]{:S(2)}) collective-permute-start(bf16[16,512]{1,0:T(8,128)(2,1)S(1)} %join_partials.1.refs_0_), channel_id=1, source_target_pairs={{0,6},{1,7},{2,4},{3,5},{4,2},{5,3},{6,0},{7,1},{8,14},{9,15},{10,... | collective-permute-start | bytes 49160 | tf_op jit(solution)/shard_map/gather_attended/ppermute | solution.py:55
  36.7 1.7 %collective-permute-start.16 = (bf16[16,512]{1,0:T(8,128)(2,1)S(1)}, bf16[16,512]{1,0:T(8,128)(2,1)S(1)}, u32[]{:S(2)}, u32[]{:S(2)}) collective-permute-start(bf16[16,512]{1,0:T(8,128)(2,1)S(1)} %join_partials.1.refs_0_), channel_id=1, source_target_pairs={{0,4},{1,5},{2,6},{3,7},{4,0},{5,1},{6,2},{7,3},{8,12},{9,13},{10,... | collective-permute-start | bytes 49160 | tf_op jit(solution)/shard_map/gather_attended/ppermute | solution.py:55
  38.4 1.6 %collective-permute-start.18 = (bf16[16,512]{1,0:T(8,128)(2,1)S(1)}, bf16[16,512]{1,0:T(8,128)(2,1)S(1)}, u32[]{:S(2)}, u32[]{:S(2)}) collective-permute-start(bf16[16,512]{1,0:T(8,128)(2,1)S(1)} %join_partials.1.refs_0_), channel_id=1, source_target_pairs={{0,2},{1,3},{2,0},{3,1},{4,6},{5,7},{6,4},{7,5},{8,10},{9,11},{10,... | collective-permute-start | bytes 49160 | tf_op jit(solution)/shard_map/gather_attended/ppermute | solution.py:55
  40.1 1.1 %collective-permute-done.14.refs_2_ = bf16[16,512]{1,0:T(8,128)(2,1)S(1)} collective-permute-done((bf16[16,512]{1,0:T(8,128)(2,1)S(1)}, bf16[16,512]{1,0:T(8,128)(2,1)S(1)}, u32[]{:S(2)}, u32[]{:S(2)}) %collective-permute-start.14) | collective-permute-done | bytes 16416 | tf_op jit(solution)/shard_map/gather_attended/ppermute | solution.py:55
  41.2 0.2 collective-permute-done.16.refs_4_
  41.4 0.3 collective-permute-start.17
  41.7 0.5 collective-permute-done.18.refs_6_
  42.3 0.1 collective-permute-done.15.refs_3_
  42.4 0.2 collective-permute-done.17.refs_5_
  42.6 0.8 %collective-permute-done.19.refs_7_ = bf16[16,512]{1,0:T(8,128)(2,1)S(1)} collective-permute-done((bf16[16,512]{1,0:T(8,128)(2,1)S(1)}, bf16[16,512]{1,0:T(8,128)(2,1)S(1)}, u32[]{:S(2)}, u32[]{:S(2)}) %collective-permute-start.19) | collective-permute-done | bytes 16416 | tf_op jit(solution)/shard_map/gather_attended/ppermute | solution.py:62
  43.4 0.6 %project_output.1 = (bf16[16,256]{1,0:T(8,128)(2,1)S(1)}, bf16[16,256]{1,0:T(8,128)(2,1)S(1)}, bf16[16,256]{1,0:T(8,128)(2,1)S(1)}, bf16[16,256]{1,0:T(8,128)(2,1)S(1)}) custom-call(s32[64,128]{1,0:T(8,128)S(1)} %get-tuple-element.22.refs_4_.tokens_ref, f32[64,8]{1,0:T(8,128)S(1)} %copy.18.logits_ref, bf16[8,512,256]{2,1,0:T(8,128)(2,1)S(1)} %copy-done, ...), custom_call_target="tpu_custom_call" | custom-call | flops 268435456 | bytes 2097152 | tf_op jit(solution)/shard_map/project_output/pallas_call | solution.py:33
  43.9 1.1 %collective-permute-start.20 = (bf16[16,256]{1,0:T(8,128)(2,1)S(1)}, bf16[16,256]{1,0:T(8,128)(2,1)S(1)}, u32[]{:S(2)}, u32[]{:S(2)}) collective-permute-start(bf16[16,256]{1,0:T(8,128)(2,1)S(1)} %get-tuple-element.36), channel_id=1, source_target_pairs={{0,24},{8,16},{16,8},{24,0},{1,25},{9,17},{17,9},{25,1},{2,26},{10... | collective-permute-start | bytes 24584 | tf_op jit(solution)/shard_map/sum_output/ppermute | solution.py:55
  45.1 0.5 %collective-permute-start.21 = (bf16[16,256]{1,0:T(8,128)(2,1)S(1)}, bf16[16,256]{1,0:T(8,128)(2,1)S(1)}, u32[]{:S(2)}, u32[]{:S(2)}) collective-permute-start(bf16[16,256]{1,0:T(8,128)(2,1)S(1)} %get-tuple-element.37), channel_id=1, source_target_pairs={{0,16},{8,24},{16,0},{24,8},{1,17},{9,25},{17,1},{25,9},{2,18},{10... | collective-permute-start | bytes 24584 | tf_op jit(solution)/shard_map/sum_output/ppermute | solution.py:55
  45.6 1.9 %collective-permute-start.22 = (bf16[16,256]{1,0:T(8,128)(2,1)S(1)}, bf16[16,256]{1,0:T(8,128)(2,1)S(1)}, u32[]{:S(2)}, u32[]{:S(2)}) collective-permute-start(bf16[16,256]{1,0:T(8,128)(2,1)S(1)} %get-tuple-element.38), channel_id=1, source_target_pairs={{0,8},{8,0},{16,24},{24,16},{1,9},{9,1},{17,25},{25,17},{2,10},{10... | collective-permute-start | bytes 24584 | tf_op jit(solution)/shard_map/sum_output/ppermute | solution.py:55
  47.5 1.1 %collective-permute-done.20.refs_1_ = bf16[16,256]{1,0:T(8,128)(2,1)S(1)} collective-permute-done((bf16[16,256]{1,0:T(8,128)(2,1)S(1)}, bf16[16,256]{1,0:T(8,128)(2,1)S(1)}, u32[]{:S(2)}, u32[]{:S(2)}) %collective-permute-start.20) | collective-permute-done | bytes 8224 | tf_op jit(solution)/shard_map/sum_output/ppermute | solution.py:55
  48.6 0.2 collective-permute-done.21.refs_2_
  48.7 0.5 %collective-permute-done.22.refs_3_ = bf16[16,256]{1,0:T(8,128)(2,1)S(1)} collective-permute-done((bf16[16,256]{1,0:T(8,128)(2,1)S(1)}, bf16[16,256]{1,0:T(8,128)(2,1)S(1)}, u32[]{:S(2)}, u32[]{:S(2)}) %collective-permute-start.22) | collective-permute-done | bytes 8224 | tf_op jit(solution)/shard_map/sum_output/ppermute | solution.py:55
  49.2 0.6 %add_output.1 = f32[16,256]{1,0:T(8,128)} custom-call(bf16[16,256]{1,0:T(8,128)(2,1)S(1)} %get-tuple-element.35.refs_0_, bf16[16,256]{1,0:T(8,128)(2,1)S(1)} %collective-permute-done.20.refs_1_, bf16[16,256]{1,0:T(8,128)(2,1)S(1)} %collective-permute-done.21.refs_2_, bf16[16,256]{1,0:T(8,128)(2,1)S(1)} %collective-permute-done.22.refs_3_), custom_call_target="tpu_custom_call" | custom-call | bytes 32768 | tf_op jit(solution)/shard_map/add_output/pallas_call | solution.py:33
  (36 shorter events, 0.6 us)
Async XLA Ops:
  0.6 6.8 %collective-permute-start = (bf16[16,256]{1,0:T(8,128)(2,1)}, bf16[16,256]{1,0:T(8,128)(2,1)S(1)}, u32[]{:S(2)}, u32[]{:S(2)}) collective-permute-start(bf16[16,256]{1,0:T(8,128)(2,1)} %refs_0_.1), channel_id=1, source_target_pairs={{0,24},{8,16},{16,8},{24,0},{1,25},{9,17},{17,9},{25,1},{2,26},{10... | collective-permute-start | bytes 24584 | tf_op jit(solution)/shard_map/gather_hidden/ppermute | solution.py:55
  4.6 3.9 %collective-permute-start.1 = (bf16[16,256]{1,0:T(8,128)(2,1)}, bf16[16,256]{1,0:T(8,128)(2,1)S(1)}, u32[]{:S(2)}, u32[]{:S(2)}) collective-permute-start(bf16[16,256]{1,0:T(8,128)(2,1)} %refs_0_.1), channel_id=1, source_target_pairs={{0,16},{8,24},{16,0},{24,8},{1,17},{9,25},{17,1},{25,9},{2,18},{10... | collective-permute-start | bytes 24584 | tf_op jit(solution)/shard_map/gather_hidden/ppermute | solution.py:55
  5.1 3.9 %collective-permute-start.2 = (bf16[16,256]{1,0:T(8,128)(2,1)}, bf16[16,256]{1,0:T(8,128)(2,1)S(1)}, u32[]{:S(2)}, u32[]{:S(2)}) collective-permute-start(bf16[16,256]{1,0:T(8,128)(2,1)} %refs_0_.1), channel_id=1, source_target_pairs={{0,8},{8,0},{16,24},{24,16},{1,9},{9,1},{17,25},{25,17},{2,10},{10... | collective-permute-start | bytes 24584 | tf_op jit(solution)/shard_map/gather_hidden/ppermute | solution.py:55
  5.2 2.1 %copy-start.3 = (bf16[256,2,512]{2,1,0:T(2,128)(2,1)S(1)}, bf16[256,2,512]{2,1,0:T(2,128)(2,1)}, u32[]{:S(2)}) copy-start(bf16[256,2,512]{2,1,0:T(2,128)(2,1)} %param.16) | copy-start | bytes 1572868
  5.2 3.7 %copy-start.1 = (bf16[8,256,512]{2,1,0:T(8,128)(2,1)S(1)}, bf16[8,256,512]{2,1,0:T(8,128)(2,1)}, u32[]{:S(2)}) copy-start(bf16[8,256,512]{2,1,0:T(8,128)(2,1)} %refs_5_.2) | copy-start | bytes 6291460
  5.2 3.7 %copy-start.2 = (bf16[16,256]{1,0:T(8,128)(2,1)S(1)}, bf16[16,256]{1,0:T(8,128)(2,1)}, u32[]{:S(2)}) copy-start(bf16[16,256]{1,0:T(8,128)(2,1)} %refs_0_.1) | copy-start | bytes 24580
  7.3 18.1 %slice-start = ((s8[8388608]{0:T(1024)(128)(4,1)}), s8[4194304]{0:T(1024)(128)(4,1)S(1)}, s32[]{:S(2)}) async-start(s8[8388608]{0:T(1024)(128)(4,1)} %bitcast.5), calls=%async_computation | async-start | bytes 8388608
  7.3 18.1 %slice-start.2 = ((s8[8388608]{0:T(1024)(128)(4,1)}), s8[4194304]{0:T(1024)(128)(4,1)S(1)}, s32[]{:S(2)}) async-start(s8[8388608]{0:T(1024)(128)(4,1)} %bitcast.7), calls=%async_computation.2 | async-start | bytes 8388608
  9.0 16.5 %slice-start.1 = ((s8[8388608]{0:T(1024)(128)(4,1)}), s8[4194304]{0:T(1024)(128)(4,1)S(1)}, s32[]{:S(2)}) async-start(s8[8388608]{0:T(1024)(128)(4,1)} %bitcast.5), calls=%async_computation.1 | async-start | bytes 8388608
  9.0 16.5 %slice-start.3 = ((s8[8388608]{0:T(1024)(128)(4,1)}), s8[4194304]{0:T(1024)(128)(4,1)S(1)}, s32[]{:S(2)}) async-start(s8[8388608]{0:T(1024)(128)(4,1)} %bitcast.7), calls=%async_computation.3 | async-start | bytes 8388608
  9.6 1.4 %collective-permute-start.3 = (bf16[4,32,512]{2,1,0:T(8,128)(2,1)S(1)}, bf16[4,32,512]{2,1,0:T(8,128)(2,1)S(1)}, u32[]{:S(2)}, u32[]{:S(2)}) collective-permute-start(bf16[4,32,512]{2,1,0:T(8,128)(2,1)S(1)} %get-tuple-element.25), channel_id=1, source_target_pairs={{0,1},{1,0},{2,3},{3,2},{4,5},{5,4},{6,7},{7,6},{8,9},{9,8},{10,11... | collective-permute-start | bytes 393224 | tf_op jit(solution)/shard_map/sum_tokens/ppermute | solution.py:62
  11.0 5.8 %collective-permute-start.4 = (bf16[32,512]{1,0:T(8,128)(2,1)S(1)}, bf16[32,512]{1,0:T(8,128)(2,1)S(1)}, u32[]{:S(2)}, u32[]{:S(2)}) collective-permute-start(bf16[32,512]{1,0:T(8,128)(2,1)S(1)} %get-tuple-element.27), channel_id=1, source_target_pairs={{0,6},{1,7},{2,4},{3,5},{4,2},{5,3},{6,0},{7,1},{8,14},{9,15},{10,... | collective-permute-start | bytes 98312 | tf_op jit(solution)/shard_map/sum_tokens/ppermute | solution.py:55
  14.7 4.8 %collective-permute-start.5 = (bf16[32,512]{1,0:T(8,128)(2,1)S(1)}, bf16[32,512]{1,0:T(8,128)(2,1)S(1)}, u32[]{:S(2)}, u32[]{:S(2)}) collective-permute-start(bf16[32,512]{1,0:T(8,128)(2,1)S(1)} %get-tuple-element.28), channel_id=1, source_target_pairs={{0,4},{1,5},{2,6},{3,7},{4,0},{5,1},{6,2},{7,3},{8,12},{9,13},{10,... | collective-permute-start | bytes 98312 | tf_op jit(solution)/shard_map/sum_tokens/ppermute | solution.py:55
  14.7 4.8 %collective-permute-start.6 = (bf16[32,512]{1,0:T(8,128)(2,1)S(1)}, bf16[32,512]{1,0:T(8,128)(2,1)S(1)}, u32[]{:S(2)}, u32[]{:S(2)}) collective-permute-start(bf16[32,512]{1,0:T(8,128)(2,1)S(1)} %get-tuple-element.29), channel_id=1, source_target_pairs={{0,2},{1,3},{2,0},{3,1},{4,6},{5,7},{6,4},{7,5},{8,10},{9,11},{10,... | collective-permute-start | bytes 98312 | tf_op jit(solution)/shard_map/sum_tokens/ppermute | solution.py:55
  19.6 22.6 %copy-start.4 = (f32[64,8]{0,1:T(8,128)S(1)}, f32[64,8]{0,1:T(8,128)}, u32[]{:S(2)}) copy-start(f32[64,8]{0,1:T(8,128)} %param.13) | copy-start | bytes 6148
  19.6 23.7 %copy-start = (bf16[8,512,256]{2,1,0:T(8,128)(2,1)S(1)}, bf16[8,512,256]{2,1,0:T(8,128)(2,1)}, u32[]{:S(2)}) copy-start(bf16[8,512,256]{2,1,0:T(8,128)(2,1)} %weight_ref.1) | copy-start | bytes 6291460
  19.6 4.7 %collective-permute-start.7 = (bf16[16,512]{1,0:T(8,128)(2,1)S(1)}, bf16[16,512]{1,0:T(8,128)(2,1)S(1)}, u32[]{:S(2)}, u32[]{:S(2)}) collective-permute-start(bf16[16,512]{1,0:T(8,128)(2,1)S(1)} %rotate_queries.1.query_ref.refs_0_), channel_id=1, source_target_pairs={{0,24},{8,16},{16,8},{24,0},{1,25},{9,17},{17,9},{25,1},{2,26},{10... | collective-permute-start | bytes 49160 | tf_op jit(solution)/shard_map/gather_queries/ppermute | solution.py:55
  21.2 3.7 %collective-permute-start.8 = (bf16[16,512]{1,0:T(8,128)(2,1)S(1)}, bf16[16,512]{1,0:T(8,128)(2,1)S(1)}, u32[]{:S(2)}, u32[]{:S(2)}) collective-permute-start(bf16[16,512]{1,0:T(8,128)(2,1)S(1)} %rotate_queries.1.query_ref.refs_0_), channel_id=1, source_target_pairs={{0,16},{8,24},{16,0},{24,8},{1,17},{9,25},{17,1},{25,9},{2,18},{10... | collective-permute-start | bytes 49160 | tf_op jit(solution)/shard_map/gather_queries/ppermute | solution.py:55
  21.7 3.7 %collective-permute-start.9 = (bf16[16,512]{1,0:T(8,128)(2,1)S(1)}, bf16[16,512]{1,0:T(8,128)(2,1)S(1)}, u32[]{:S(2)}, u32[]{:S(2)}) collective-permute-start(bf16[16,512]{1,0:T(8,128)(2,1)S(1)} %rotate_queries.1.query_ref.refs_0_), channel_id=1, source_target_pairs={{0,8},{8,0},{16,24},{24,16},{1,9},{9,1},{17,25},{25,17},{2,10},{10... | collective-permute-start | bytes 49160 | tf_op jit(solution)/shard_map/gather_queries/ppermute | solution.py:55
  28.6 4.9 %collective-permute-start.10 = (bf16[16,640]{1,0:T(8,128)(2,1)S(1)}, bf16[16,640]{1,0:T(8,128)(2,1)S(1)}, u32[]{:S(2)}, u32[]{:S(2)}) collective-permute-start(bf16[16,640]{1,0:T(8,128)(2,1)S(1)} %get-tuple-element.32), channel_id=1, source_target_pairs={{0,24},{8,16},{16,8},{24,0},{1,25},{9,17},{17,9},{25,1},{2,26},{10... | collective-permute-start | bytes 61448 | tf_op jit(solution)/shard_map/trade_partials/ppermute | solution.py:55
  31.1 3.8 %collective-permute-start.11 = (bf16[16,640]{1,0:T(8,128)(2,1)S(1)}, bf16[16,640]{1,0:T(8,128)(2,1)S(1)}, u32[]{:S(2)}, u32[]{:S(2)}) collective-permute-start(bf16[16,640]{1,0:T(8,128)(2,1)S(1)} %get-tuple-element.33), channel_id=1, source_target_pairs={{0,16},{8,24},{16,0},{24,8},{1,17},{9,25},{17,1},{25,9},{2,18},{10... | collective-permute-start | bytes 61448 | tf_op jit(solution)/shard_map/trade_partials/ppermute | solution.py:55
  31.6 3.8 %collective-permute-start.12 = (bf16[16,640]{1,0:T(8,128)(2,1)S(1)}, bf16[16,640]{1,0:T(8,128)(2,1)S(1)}, u32[]{:S(2)}, u32[]{:S(2)}) collective-permute-start(bf16[16,640]{1,0:T(8,128)(2,1)S(1)} %get-tuple-element.34), channel_id=1, source_target_pairs={{0,8},{8,0},{16,24},{24,16},{1,9},{9,1},{17,25},{25,17},{2,10},{10... | collective-permute-start | bytes 61448 | tf_op jit(solution)/shard_map/trade_partials/ppermute | solution.py:55
  35.6 5.6 %collective-permute-start.14 = (bf16[16,512]{1,0:T(8,128)(2,1)S(1)}, bf16[16,512]{1,0:T(8,128)(2,1)S(1)}, u32[]{:S(2)}, u32[]{:S(2)}) collective-permute-start(bf16[16,512]{1,0:T(8,128)(2,1)S(1)} %join_partials.1.refs_0_), channel_id=1, source_target_pairs={{0,6},{1,7},{2,4},{3,5},{4,2},{5,3},{6,0},{7,1},{8,14},{9,15},{10,... | collective-permute-start | bytes 49160 | tf_op jit(solution)/shard_map/gather_attended/ppermute | solution.py:55
  36.7 4.7 %collective-permute-start.16 = (bf16[16,512]{1,0:T(8,128)(2,1)S(1)}, bf16[16,512]{1,0:T(8,128)(2,1)S(1)}, u32[]{:S(2)}, u32[]{:S(2)}) collective-permute-start(bf16[16,512]{1,0:T(8,128)(2,1)S(1)} %join_partials.1.refs_0_), channel_id=1, source_target_pairs={{0,4},{1,5},{2,6},{3,7},{4,0},{5,1},{6,2},{7,3},{8,12},{9,13},{10,... | collective-permute-start | bytes 49160 | tf_op jit(solution)/shard_map/gather_attended/ppermute | solution.py:55
  38.4 3.7 %collective-permute-start.18 = (bf16[16,512]{1,0:T(8,128)(2,1)S(1)}, bf16[16,512]{1,0:T(8,128)(2,1)S(1)}, u32[]{:S(2)}, u32[]{:S(2)}) collective-permute-start(bf16[16,512]{1,0:T(8,128)(2,1)S(1)} %join_partials.1.refs_0_), channel_id=1, source_target_pairs={{0,2},{1,3},{2,0},{3,1},{4,6},{5,7},{6,4},{7,5},{8,10},{9,11},{10,... | collective-permute-start | bytes 49160 | tf_op jit(solution)/shard_map/gather_attended/ppermute | solution.py:55
  40.1 2.2 %collective-permute-start.13 = (bf16[16,512]{1,0:T(8,128)(2,1)S(1)}, bf16[16,512]{1,0:T(8,128)(2,1)S(1)}, u32[]{:S(2)}, u32[]{:S(2)}) collective-permute-start(bf16[16,512]{1,0:T(8,128)(2,1)S(1)} %join_partials.1.refs_0_), channel_id=1, source_target_pairs={{0,1},{1,0},{2,3},{3,2},{4,5},{5,4},{6,7},{7,6},{8,9},{9,8},{10,11... | collective-permute-start | bytes 49160 | tf_op jit(solution)/shard_map/gather_attended/ppermute | solution.py:62
  41.2 1.2 %collective-permute-start.15 = (bf16[16,512]{1,0:T(8,128)(2,1)S(1)}, bf16[16,512]{1,0:T(8,128)(2,1)S(1)}, u32[]{:S(2)}, u32[]{:S(2)}) collective-permute-start(bf16[16,512]{1,0:T(8,128)(2,1)S(1)} %collective-permute-done.14.refs_2_), channel_id=1, source_target_pairs={{0,1},{1,0},{2,3},{3,2},{4,5},{5,4},{6,7},{7,6},{8,9},{9,8},{10,11... | collective-permute-start | bytes 49160 | tf_op jit(solution)/shard_map/gather_attended/ppermute | solution.py:62
  41.4 1.2 %collective-permute-start.17 = (bf16[16,512]{1,0:T(8,128)(2,1)S(1)}, bf16[16,512]{1,0:T(8,128)(2,1)S(1)}, u32[]{:S(2)}, u32[]{:S(2)}) collective-permute-start(bf16[16,512]{1,0:T(8,128)(2,1)S(1)} %collective-permute-done.16.refs_4_), channel_id=1, source_target_pairs={{0,1},{1,0},{2,3},{3,2},{4,5},{5,4},{6,7},{7,6},{8,9},{9,8},{10,11... | collective-permute-start | bytes 49160 | tf_op jit(solution)/shard_map/gather_attended/ppermute | solution.py:62
  42.2 1.2 %collective-permute-start.19 = (bf16[16,512]{1,0:T(8,128)(2,1)S(1)}, bf16[16,512]{1,0:T(8,128)(2,1)S(1)}, u32[]{:S(2)}, u32[]{:S(2)}) collective-permute-start(bf16[16,512]{1,0:T(8,128)(2,1)S(1)} %collective-permute-done.18.refs_6_), channel_id=1, source_target_pairs={{0,1},{1,0},{2,3},{3,2},{4,5},{5,4},{6,7},{7,6},{8,9},{9,8},{10,11... | collective-permute-start | bytes 49160 | tf_op jit(solution)/shard_map/gather_attended/ppermute | solution.py:62
  43.9 4.6 %collective-permute-start.20 = (bf16[16,256]{1,0:T(8,128)(2,1)S(1)}, bf16[16,256]{1,0:T(8,128)(2,1)S(1)}, u32[]{:S(2)}, u32[]{:S(2)}) collective-permute-start(bf16[16,256]{1,0:T(8,128)(2,1)S(1)} %get-tuple-element.36), channel_id=1, source_target_pairs={{0,24},{8,16},{16,8},{24,0},{1,25},{9,17},{17,9},{25,1},{2,26},{10... | collective-permute-start | bytes 24584 | tf_op jit(solution)/shard_map/sum_output/ppermute | solution.py:55
  45.1 3.7 %collective-permute-start.21 = (bf16[16,256]{1,0:T(8,128)(2,1)S(1)}, bf16[16,256]{1,0:T(8,128)(2,1)S(1)}, u32[]{:S(2)}, u32[]{:S(2)}) collective-permute-start(bf16[16,256]{1,0:T(8,128)(2,1)S(1)} %get-tuple-element.37), channel_id=1, source_target_pairs={{0,16},{8,24},{16,0},{24,8},{1,17},{9,25},{17,1},{25,9},{2,18},{10... | collective-permute-start | bytes 24584 | tf_op jit(solution)/shard_map/sum_output/ppermute | solution.py:55
  45.6 3.7 %collective-permute-start.22 = (bf16[16,256]{1,0:T(8,128)(2,1)S(1)}, bf16[16,256]{1,0:T(8,128)(2,1)S(1)}, u32[]{:S(2)}, u32[]{:S(2)}) collective-permute-start(bf16[16,256]{1,0:T(8,128)(2,1)S(1)} %get-tuple-element.38), channel_id=1, source_target_pairs={{0,8},{8,0},{16,24},{24,16},{1,9},{9,1},{17,25},{25,17},{2,10},{10... | collective-permute-start | bytes 24584 | tf_op jit(solution)/shard_map/sum_output/ppermute | solution.py:55
